TPU v7x, 32 devices: a whole 2x2x4 slice. The times are simulated.
32 devices in a mesh: groups: 2 (over y), tp: 16 (over z, x, core).
Axes of the slice: x: 2, y: 2, z: 4, core: 2. Of those that a mesh axis runs over, the one named last changes fastest.
Arguments:
- hidden: bfloat16 [16384, 8192], P(('groups', 'tp')), parts along dimension 0, may hold values from -8 to 8
- norm_gain: float32 [8192], replicated, may hold values from 0.1 to 1.9
- w_query: bfloat16 [8192, 4096], P('tp'), may hold values from -0.25 to 0.25
- b_query: float32 [4096], replicated, may hold values from -3 to 3
- w_key: bfloat16 [8192, 512], P('tp'), may hold values from -0.0677561 to 0.0677561
- w_value: bfloat16 [8192, 512], P('tp'), may hold values from -0.0625 to 0.0625
- b_value: float32 [512], replicated, may hold values from -4 to 4
- w_out: bfloat16 [4096, 8192], P('tp'), may hold values from -0.09375 to 0.09375
- step_ends: int32 [32], P('groups'), parts along dimension 0, may hold values from 0 to 8191, as said below
Outputs:
- scored_out: bfloat16 [32, 8192], P(('groups', 'tp')), parts along dimension 0
There are 2 independent parts, one for each index of `groups`. A program takes and returns all parts, laid end to end along the dimension named above; an argument that names none is the same for every part. Nothing has to cross between parts.
Inputs may be any that keep to these rules, and one draw needn't show every extreme that they name: `step_ends`: entry i lies among tokens 512 * i to 512 * (i + 1) - 1; the last entry is the trace's last token.
All inputs are finite; a program needn't handle non-finite values.
Results may differ from a plain program's by a relative error of at most 0.012.
The roundings to bfloat16 on the way count: a program that leaves them out, or rounds other values in their place, can miss the bound.
Values may be sent and summed in bfloat16 or wider, within the bound.
A program may use at most 128 MiB of HBM per device.

v0:
```python
import jax
import jax.numpy as jnp
from jax import lax
from jax.sharding import PartitionSpec as P

HEADS = 32
KV = 4
HEAD = 128


def normed(rows, norm_gain):
    widened = rows.astype(jnp.float32)
    inverse_rms = lax.rsqrt(jnp.mean(widened * widened, axis=-1, keepdims=True) + 1e-06)
    return (widened * inverse_rms * norm_gain).astype(jnp.bfloat16)


def shards(hidden, norm_gain, w_query, b_query, w_key, w_value, b_value, w_out, step_ends):
    devices = lax.axis_size("tp")
    device_index = lax.axis_index("tp")
    tok_rows = hidden.shape[0]
    scored_count = step_ends.shape[0]
    per_owner = scored_count // devices
    group_ratio = HEADS // KV
    normal_rows = normed(hidden, norm_gain)
    key_sum = jnp.dot(
        normal_rows,
        lax.all_gather(w_key, "tp", axis=0, tiled=True),
        preferred_element_type=jnp.float32,
    )
    value_sum = jnp.dot(
        normal_rows,
        lax.all_gather(w_value, "tp", axis=0, tiled=True),
        preferred_element_type=jnp.float32,
    )
    key_rows = key_sum.astype(jnp.bfloat16)
    value_rows = (value_sum + b_value).astype(jnp.bfloat16)
    own_positions = lax.dynamic_slice_in_dim(step_ends, device_index * per_owner, per_owner, 0)
    own_offsets = own_positions - device_index * tok_rows
    own_scored = jnp.take(normal_rows, own_offsets, axis=0)
    scored_cols = lax.all_to_all(own_scored, "tp", split_axis=1, concat_axis=0, tiled=True)
    partial_query = jnp.dot(scored_cols, w_query, preferred_element_type=jnp.float32)
    queries = (lax.psum(partial_query, "tp") + b_query).astype(jnp.bfloat16)
    query_blocks = queries.reshape(scored_count, KV, group_ratio, HEAD)
    key_blocks = key_rows.reshape(tok_rows, KV, HEAD)
    value_blocks = value_rows.reshape(tok_rows, KV, HEAD)
    scores = jnp.einsum(
        "sgrd,tgd->sgrt", query_blocks, key_blocks, preferred_element_type=jnp.float32
    ) * HEAD ** (-0.5)
    key_positions = device_index * tok_rows + jnp.arange(tok_rows, dtype=jnp.int32)
    visible = key_positions[None, None, None, :] <= step_ends[:, None, None, None]
    scores = jnp.where(visible, scores, -1e30)
    local_peak = jnp.max(scores, axis=3)
    global_peak = lax.pmax(local_peak, "tp")
    weights = jnp.where(visible, jnp.exp(scores - global_peak[..., None]), 0.0)
    denominator = jnp.sum(weights, axis=3)
    summed = jnp.einsum(
        "sgrt,tgd->sgrd",
        weights.astype(jnp.bfloat16),
        value_blocks,
        preferred_element_type=jnp.float32,
    )
    owner_sum, owner_total = (
        lax.psum_scatter(
            summed.reshape(scored_count, HEADS * HEAD), "tp", scatter_dimension=0, tiled=True
        ),
        lax.psum_scatter(
            denominator.reshape(scored_count, HEADS), "tp", scatter_dimension=0, tiled=True
        ),
    )
    attended = owner_sum.reshape(per_owner, HEADS, HEAD) / owner_total[..., None]
    mixed_row = attended.reshape(per_owner, HEADS * HEAD).astype(jnp.bfloat16)
    mixed_cols = lax.all_to_all(mixed_row, "tp", split_axis=1, concat_axis=0, tiled=True)
    return lax.psum_scatter(
        jnp.dot(mixed_cols, w_out, preferred_element_type=jnp.float32),
        "tp",
        scatter_dimension=0,
        tiled=True,
    ).astype(jnp.bfloat16)


def solution(mesh):
    in_specs = (
        P(("groups", "tp"), None),
        P(),
        P("tp", None),
        P(),
        P("tp", None),
        P("tp", None),
        P(),
        P("tp", None),
        P("groups"),
    )
    out_specs = P(("groups", "tp"), None)
    return jax.shard_map(shards, mesh=mesh, in_specs=in_specs, out_specs=out_specs, check_vma=False)
```

profile of v0, /device:TPU:0, one launch (start us, length us, event | category | flops | bytes accessed | tf_op | source)
XLA Modules:
  0.0 469.4 jit_solution(7079866566982820845)
XLA Ops:
  6.5 0.0 all-reduce.7.cloned.1.call-start
  6.5 1.2 dynamic_slice.3
  8.4 5.1 %fusion = f32[512]{0:T(512)S(1)} fusion(bf16[512,8192]{1,0:T(8,128)(2,1)} %param.9), kind=kLoop, calls=%fused_computation.2 | loop fusion | flops 12582400 | bytes 8390656 | tf_op jit(solution)/shard_map/reduce_sum | solution.py:13
  13.6 0.0 copy-done
  13.6 0.0 copy-start.4
  13.6 0.0 copy-start.2
  13.6 0.0 copy-start.1
  13.6 9.9 %fusion.2 = bf16[512,8192]{1,0:T(8,128)(2,1)} fusion(bf16[512,8192]{1,0:T(8,128)(2,1)} %param.9, f32[8192]{0:T(1024)S(1)} %copy-done, f32[512]{0:T(512)S(1)} %add_rsqrt_fusion), kind=kLoop, calls=%fused_computation.4 | loop fusion | flops 16777216 | bytes 16812032 | tf_op jit(solution)/shard_map/convert_element_type | solution.py:14
  23.5 0.9 broadcast_select_fusion
  24.4 0.5 broadcast.83
  24.9 0.7 reduce.2
  25.7 13.7 %all_to_all.29 = bf16[16,2,256]{2,1,0:T(2,128)(2,1)S(1)} all-to-all(bf16[16,2,256]{2,1,0:T(2,128)(2,1)S(1)} %reshape.149), channel_id=1, replica_groups=mesh['groups'=2,'tp'=16] {'tp'}, dimensions={0} | all-to-all | bytes 32768 | tf_op jit(solution)/shard_map/all_to_all | solution.py:40
  39.4 3.6 fusion.14
  42.9 0.0 all-reduce.7.cloned.1.call-update
  42.9 0.0 all-gather.5.cloned.1.call-start
  43.0 0.7 all-gather.5.cloned.1.call-update
  43.7 0.0 all-gather.3.cloned.1.call-start
  43.7 0.7 all-gather.3.cloned.1.call-update
  44.4 0.0 all-reduce.9.cloned.1.call-start
  44.5 0.0 copy-done.4
  44.5 0.6 dynamic-slice.4
  45.1 0.0 copy-done.2
  45.1 0.1 broadcast_compare_fusion
  45.2 84.0 %all-reduce.7.cloned.1.call-done = f32[16,4096]{1,0:T(8,128)} async-done(((f32[16,4096]{1,0:T(8,128)}), f32[16,4096]{1,0:T(8,128)}) %all-reduce.7.cloned.1.call-update) | async-done | bytes 262160 | tf_op jit(solution)/shard_map/psum | solution.py:42
  129.2 0.0 copy-done.1
  129.2 1.0 fusion.12
  130.2 0.0 copy-start.3
  130.2 76.6 %all-gather.5.cloned.1.call-done = bf16[8192,512]{1,0:T(8,128)(2,1)} async-done(((bf16[512,512]{1,0:T(8,128)(2,1)}), bf16[8192,512]{1,0:T(8,128)(2,1)}) %all-gather.5.cloned.1.call-update) | async-done | bytes 8388624 | tf_op jit(solution)/shard_map/all_gather | solution.py:27
  206.8 10.3 %convolution_convert_fusion = bf16[512,512]{0,1:T(8,128)(2,1)S(1)} fusion(bf16[512,8192]{1,0:T(8,128)(2,1)} %fusion.2, bf16[8192,512]{1,0:T(8,128)(2,1)} %all-gather.5.cloned.1.call-done), kind=kOutput, calls=%fused_computation.10 | convolution fusion | flops 4295229440 | bytes 17301504 | tf_op jit(solution)/shard_map/dot_general | solution.py:25
  217.1 0.4 fusion.22
  217.5 60.7 %pmax.7 = f32[16,4,8]{0,2,1:T(8,128)S(1)} all-reduce(f32[16,4,8]{0,2,1:T(8,128)S(1)} %get-tuple-element.16), channel_id=1, replica_groups=mesh['groups'=2,'tp'=16] {'tp'}, use_global_device_ids=true, to_apply=%region_3.4 | all-reduce | flops 512 | bytes 4096 | tf_op jit(solution)/shard_map/pmax | solution.py:53
  278.2 4.8 %all-gather.3.cloned.1.call-done = bf16[8192,512]{1,0:T(8,128)(2,1)} async-done(((bf16[512,512]{1,0:T(8,128)(2,1)}), bf16[8192,512]{1,0:T(8,128)(2,1)}) %all-gather.3.cloned.1.call-update) | async-done | bytes 8388624 | tf_op jit(solution)/shard_map/all_gather | solution.py:32
  283.0 10.3 %fusion.5 = bf16[512,512]{0,1:T(8,128)(2,1)S(1)} fusion(bf16[512,8192]{1,0:T(8,128)(2,1)} %fusion.2, bf16[8192,512]{1,0:T(8,128)(2,1)} %all-gather.3.cloned.1.call-done, f32[512]{0:T(512)S(1)} %copy-done.3), kind=kOutput, calls=%fused_computation.9 | convolution fusion | flops 4295491584 | bytes 17303552 | tf_op jit(solution)/shard_map/dot_general | solution.py:30
  293.3 0.4 convolution_bitcast_fusion
  293.7 0.1 copy.29
  293.8 0.9 copy.56
  294.7 0.0 all-reduce.9.cloned.1.call-update
  294.7 0.3 fusion.6
  295.0 59.1 %all-reduce.1 = f32[16,32]{0,1:T(8,128)S(1)} all-reduce(f32[16,32]{0,1:T(8,128)S(1)} %bitcast.59), channel_id=3, replica_groups=mesh['groups'=2,'tp'=16] {'tp'}, use_global_device_ids=true, to_apply=%region_6.7.clone | all-reduce | flops 512 | bytes 4096
  354.1 0.8 dynamic-slice_reduce_fusion
  354.9 27.0 %all-reduce.9.cloned.1.call-done = f32[16,4096]{1,0:T(8,128)} async-done(((f32[16,4096]{1,0:T(8,128)}), f32[16,4096]{1,0:T(8,128)}) %all-reduce.9.cloned.1.call-update) | async-done | bytes 262160
  381.9 0.1 div.22
  382.0 1.6 fusion.17
  383.6 0.7 reduce.3
  384.3 11.4 %all_to_all.30 = bf16[16,2,128]{2,1,0:T(2,128)(2,1)S(1)} all-to-all(bf16[16,2,128]{2,1,0:T(2,128)(2,1)S(1)} %reshape.151), channel_id=1, replica_groups=mesh['groups'=2,'tp'=16] {'tp'}, dimensions={0} | all-to-all | bytes 16384 | tf_op jit(solution)/shard_map/all_to_all | solution.py:72
  395.7 2.8 fusion.18
  398.6 63.0 %all-reduce.10 = bf16[16,8192]{1,0:T(8,128)(2,1)S(1)} all-reduce(f32[16,8192]{1,0:T(8,128)S(1)} %fusion.18), channel_id=4, replica_groups=mesh['groups'=2,'tp'=16] {'tp'}, use_global_device_ids=true, to_apply=%region_7.8.clone | all-reduce | flops 131072 | bytes 786432
  461.5 1.3 dynamic-slice_convert_fusion
  (9 shorter events, 0.1 us)
Async XLA Ops:
  6.5 7.0 %copy-start = (f32[8192]{0:T(1024)S(1)}, f32[8192]{0:T(1024)}, u32[]{:S(2)}) copy-start(f32[8192]{0:T(1024)} %param.10) | copy-start | bytes 98308
  6.5 122.7 %all-reduce.7.cloned.1.call-start = ((), (), s32[]{:S(2)}) async-start(), calls=%async_computation.4 | async-start | bytes 524288 | tf_op jit(solution)/shard_map/psum | solution.py:42
  13.6 30.9 %copy-start.4 = (u32[32]{0:T(128)S(1)}, u32[32]{0:T(128)}, u32[]{:S(2)}) copy-start(u32[32]{0:T(128)} %constant.63) | copy-start | bytes 388
  13.6 31.5 %copy-start.2 = (s32[16]{0:T(128)S(1)}, s32[16]{0:T(128)}, u32[]{:S(2)}) copy-start(s32[16]{0:T(128)} %param.17) | copy-start | bytes 196
  13.6 115.6 %copy-start.1 = (f32[4096]{0:T(1024)S(1)}, f32[4096]{0:T(1024)}, u32[]{:S(2)}) copy-start(f32[4096]{0:T(1024)} %param.12) | copy-start | bytes 49156
  42.9 163.9 %all-gather.5.cloned.1.call-start = ((), (), s32[]{:S(2)}) async-start(), calls=%async_computation.3 | async-start | bytes 8912896 | tf_op jit(solution)/shard_map/all_gather | solution.py:27
  43.7 239.3 %all-gather.3.cloned.1.call-start = ((), (), s32[]{:S(2)}) async-start(), calls=%async_computation.2 | async-start | bytes 8912896 | tf_op jit(solution)/shard_map/all_gather | solution.py:32
  44.4 337.5 %all-reduce.9.cloned.1.call-start = ((), (), s32[]{:S(2)}) async-start(), calls=%async_computation.5 | async-start | bytes 524288
  130.2 152.8 %copy-start.3 = (f32[512]{0:T(512)S(1)}, f32[512]{0:T(512)}, u32[]{:S(2)}) copy-start(f32[512]{0:T(512)} %param.15) | copy-start | bytes 6148
Sparse Core Ops, SparseCore 0:
  43.1 86.1 all-reduce.6
  131.4 75.3 all-gather.4
  209.0 73.9 all-gather.2
  294.8 87.0 all-reduce.8
where the time goes:
time: 470 us; the launch traced here: 469 us
  blocking collectives  208 us (44%)
  waiting for transfers between devices  194 us (41%)
  matrix products  27.7 us (6%)
  other arithmetic  20.3 us (4%)
  between operations  13.9 us (3%)
  local copies, waits for them, and re-layouts  5.6 us (1%)
    unnamed x2, blocking collectives  122 us
    psum x1, waiting for transfers between devices, shards(): queries = (lax.psum(partial_query, 'tp') + b_query).astype(jnp.bfloat16)  84 us
    all_gather x1, waiting for transfers between devices, shards(): lax.all_gather(w_key, 'tp', axis=0, tiled=True)  76.6 us
    pmax x1, blocking collectives, shards(): global_peak = lax.pmax(local_peak, 'tp')  60.7 us
    unnamed x5, waiting for transfers between devices  28.4 us
    all_to_all x1, blocking collectives, shards(): lax.all_to_all(own_scored, 'tp', split_axis=1, concat_axis=0, tiled=True)  13.7 us
    all_to_all x1, blocking collectives, shards(): lax.all_to_all(mixed_row, 'tp', split_axis=1, concat_axis=0, tiled=True)  11.4 us
    dot_general x1, matrix products, shards(): jnp.dot(normal_rows, lax.all_gather(w_value, 'tp', axis=0, tiled=True), p...  10.3 us
  transfers between devices with their start and end apart: 4, of which 4 were waited for; matrix products, arithmetic and copies ran while one was open for 3% of the time, Pallas kernels for 0%

commit v1 on v0

--- a/solution.py
+++ b/solution.py
@@ -1,11 +1,14 @@
 import jax
 import jax.numpy as jnp
 from jax import lax
+from jax.experimental import pallas as pl
+from jax.experimental.pallas import tpu as pltpu
 from jax.sharding import PartitionSpec as P
 
 HEADS = 32
 KV = 4
 HEAD = 128
+MESH = pl.DeviceIdType.MESH
 
 
 def normed(rows, norm_gain):
@@ -78,6 +81,426 @@
     ).astype(jnp.bfloat16)
 
 
+RING = 8
+SPLIT = 176
+NORM_ROWS = 32
+
+
+def kernel(
+    row_ref, ends_ref, gain_ref, bq_ref, bv_ref, hidden_ref, wq_hbm, wk_hbm, wv_hbm, wo_hbm,
+    out_ref,
+    normal, held, acc, wq, wo, row_send, row_recv, cols, pq_send, pq_recv, q_all,
+    o_send, o_recv, l_send, l_recv, lmat, tmat, f_rows, f_send, f_recv,
+    load_sem, ring_send, ring_recv, y_send, y_recv, core_send, core_recv,
+    a2a_send, a2a_recv,
+):
+    n = 16
+    me = lax.axis_index("tp")
+    y = lax.axis_index("groups")
+    core = me % 2
+    chip = me // 2
+    x = chip % 2
+    z = chip // 2
+    pos = z * (1 - x) + (RING - 1 - z) * x
+    partner = chip * 2 + 1 - core
+    block = wk_hbm.shape[0]
+    ring_rows = pl.ds(pl.multiple_of(y * SPLIT, 16), block - SPLIT)
+    y_rows = pl.ds(pl.multiple_of(y * (block - SPLIT), 16), SPLIT)
+    w_hbm = (wk_hbm, wv_hbm)
+
+    def chip_at(p):
+        p = (p + 2 * RING) % RING
+        far = p // (RING // 2)
+        return (1 - far) * (2 * p) + far * (2 * RING - 1 - 2 * p)
+
+    def origin(d, k, c):
+        return chip_at(pos + (2 * d - 1) * k) * 2 + c
+
+    def ring_copy(d, k, src=None):
+        slot = origin(d, k, core)
+        return pltpu.make_async_remote_copy(
+            src_ref=held.at[d, slot, ring_rows] if src is None else src.at[ring_rows],
+            dst_ref=held.at[d, slot, ring_rows],
+            send_sem=ring_send.at[d, k],
+            recv_sem=ring_recv.at[d, k],
+            device_id={"tp": chip_at(pos + (1 - 2 * d)) * 2 + core},
+            device_id_type=MESH,
+        )
+
+    def ring_arrival(d, k):
+        slot = origin(d, k + 1, core)
+        return pltpu.make_async_remote_copy(
+            src_ref=held.at[d, slot, ring_rows],
+            dst_ref=held.at[d, slot, ring_rows],
+            send_sem=ring_send.at[d, k],
+            recv_sem=ring_recv.at[d, k],
+            device_id={"tp": chip_at(pos + (1 - 2 * d)) * 2 + core},
+            device_id_type=MESH,
+        )
+
+    def y_copy(d, k, rows):
+        slot = origin(d, k, core)
+        return pltpu.make_async_remote_copy(
+            src_ref=held.at[d, slot, rows],
+            dst_ref=held.at[d, slot, rows],
+            send_sem=y_send.at[d, k],
+            recv_sem=y_recv.at[d, k],
+            device_id={"groups": 1 - y},
+            device_id_type=MESH,
+        )
+
+    peer_rows = pl.ds(pl.multiple_of((1 - y) * (block - SPLIT), 16), SPLIT)
+
+    def core_copy(d, k, c, src=None):
+        slot = origin(d, k, c)
+        return pltpu.make_async_remote_copy(
+            src_ref=held.at[d, slot] if src is None else src,
+            dst_ref=held.at[d, slot],
+            send_sem=core_send.at[d, k],
+            recv_sem=core_recv.at[d, k],
+            device_id={"tp": partner},
+            device_id_type=MESH,
+        )
+
+    def peer_copy(phase, peer, slot, send, recv):
+        return pltpu.make_async_remote_copy(
+            src_ref=send,
+            dst_ref=recv.at[slot],
+            send_sem=a2a_send.at[phase, peer],
+            recv_sem=a2a_recv.at[phase, slot],
+            device_id={"tp": peer},
+            device_id_type=MESH,
+        )
+
+    def for_peers(body):
+        @pl.loop(1, n)
+        def _(k):
+            body((me + k) % n)
+
+    def exchange(phase, send_of, recv):
+        for_peers(lambda peer: peer_copy(phase, peer, me, send_of(peer), recv).start())
+
+    def arrive(phase, send_of, recv):
+        for_peers(lambda peer: peer_copy(phase, peer, peer, send_of(peer), recv).wait_recv())
+
+    def sent(phase, send_of, recv):
+        for_peers(lambda peer: peer_copy(phase, peer, me, send_of(peer), recv).wait_send())
+
+    loads = [
+        pltpu.make_async_copy(hidden_ref, normal, load_sem.at[0]),
+        pltpu.make_async_copy(wq_hbm, wq, load_sem.at[1]),
+        pltpu.make_async_copy(wk_hbm, held.at[0, me], load_sem.at[2]),
+        pltpu.make_async_copy(wv_hbm, held.at[1, me], load_sem.at[3]),
+        pltpu.make_async_copy(wo_hbm, wo, load_sem.at[4]),
+    ]
+    for load in loads:
+        load.start()
+
+    barrier = pltpu.get_barrier_semaphore()
+    for_peers(
+        lambda peer: pl.semaphore_signal(
+            barrier, inc=1, device_id={"tp": peer}, device_id_type=MESH
+        )
+    )
+    pl.semaphore_signal(barrier, inc=1, device_id={"groups": 1 - y}, device_id_type=MESH)
+    pl.semaphore_wait(barrier, n)
+
+    for d in range(2):
+        ring_copy(d, 0, w_hbm[d]).start()
+    for d in range(2):
+        core_copy(d, 0, core, w_hbm[d]).start()
+
+    row = row_ref[...]
+    row_scale = lax.rsqrt(jnp.sum(row * row, axis=-1, keepdims=True) / row.shape[1] + 1e-06)
+    for j in range(n):
+        part = pl.ds(j * block, block)
+        piece = row_ref[:, part] * row_scale * gain_ref[:, part]
+        row_send[j] = piece.astype(jnp.bfloat16).astype(jnp.float32)
+    row_recv[pl.ds(me, 1)] = row_send[pl.ds(me, 1)]
+    row_of = lambda peer: row_send.at[peer]
+    exchange(0, row_of, row_recv)
+    for load in loads:
+        load.wait()
+
+    width = normal.shape[1]
+    piece_lanes = 256
+
+    def norm_rows(first, last):
+        @pl.loop(first, last)
+        def _(i):
+            rows = pl.ds(pl.multiple_of(i * NORM_ROWS, NORM_ROWS), NORM_ROWS)
+            squares = jnp.zeros((NORM_ROWS, piece_lanes), jnp.float32)
+            for c in range(0, width, piece_lanes):
+                v = normal[rows, pl.ds(c, piece_lanes)].astype(jnp.float32)
+                squares = squares + v * v
+            scale = lax.rsqrt(jnp.sum(squares, axis=-1, keepdims=True) / width + 1e-06)
+            for c in range(0, width, piece_lanes):
+                lanes = pl.ds(c, piece_lanes)
+                v = normal[rows, lanes].astype(jnp.float32)
+                normal[rows, lanes] = (v * scale * gain_ref[:, lanes]).astype(jnp.bfloat16)
+
+    tok_rows = normal.shape[0]
+    steps = tok_rows // NORM_ROWS
+    norm_rows(0, steps // 2)
+    acc[...] = jnp.zeros_like(acc)
+
+    def project(k, c):
+        @pl.loop(0, 2)
+        def _(d):
+            slot = origin(d, k, c)
+            lanes = pl.ds(pl.multiple_of(slot * block, block), block)
+            acc[d] += jnp.dot(
+                normal[:, lanes], held[d, slot], preferred_element_type=jnp.float32
+            )
+
+    share = wq.shape[1] // n
+    pq_of = lambda peer: pq_send.at[peer]
+    q_of = lambda peer: q_all.at[me]
+
+    @pl.loop(0, RING - 1)
+    def _(s):
+        for d in range(2):
+            ring_arrival(d, s).wait_recv()
+
+            @pl.when(s < RING - 2)
+            def _():
+                ring_copy(d, s + 1).start()
+
+            y_copy(d, s + 1, y_rows).start()
+
+        @pl.when(s >= 1)
+        def _():
+            for d in range(2):
+                y_copy(d, s, peer_rows).wait_recv()
+                core_copy(d, s, core).start()
+
+        @pl.when(s == 0)
+        def _():
+            arrive(0, row_of, row_recv)
+            for j in range(n):
+                cols[j : j + 1, :] = row_recv[j]
+            scored = cols[...].astype(jnp.bfloat16)
+
+            @pl.loop(0, n)
+            def _(j):
+                pq_send[j] = jnp.dot(
+                    scored,
+                    wq[:, pl.ds(pl.multiple_of(j * share, share), share)],
+                    preferred_element_type=jnp.float32,
+                )
+
+            pq_recv[pl.ds(me, 1)] = pq_send[pl.ds(me, 1)]
+            exchange(1, pq_of, pq_recv)
+            norm_rows(steps // 2, steps)
+            project(0, core)
+
+        @pl.when(s == 1)
+        def _():
+            arrive(1, pq_of, pq_recv)
+            total = pq_recv[0]
+            for j in range(1, n):
+                total = total + pq_recv[j]
+            bias = bq_ref[:, pl.ds(pl.multiple_of(me * share, share), share)]
+            q_all[me] = (total + bias).astype(jnp.bfloat16)
+            exchange(2, q_of, q_all)
+
+        @pl.when(s >= 1)
+        def _():
+            project(s, core)
+            for d in range(2):
+                core_copy(d, s - 1, 1 - core).wait_recv()
+            project(s - 1, 1 - core)
+
+    for d in range(2):
+        y_copy(d, RING - 1, peer_rows).wait_recv()
+        core_copy(d, RING - 1, core).start()
+    project(RING - 1, core)
+    for k in (RING - 2, RING - 1):
+        for d in range(2):
+            core_copy(d, k, 1 - core).wait_recv()
+        project(k, 1 - core)
+
+    arrive(2, q_of, q_all)
+    key_rows = acc[0].astype(jnp.bfloat16)
+    value_rows = (acc[1] + bv_ref[...]).astype(jnp.bfloat16)
+    scored_count = n
+    group_rows = scored_count * (HEADS // KV)
+    per_group = n // KV
+    row_of_score = lax.broadcasted_iota(jnp.int32, (group_rows, 1), 0) % scored_count
+    limit = jnp.zeros((group_rows, 1), jnp.int32)
+    for j in range(scored_count):
+        limit = jnp.where(row_of_score == j, ends_ref[j], limit)
+    token = lax.broadcasted_iota(jnp.int32, (group_rows, tok_rows), 1) + me * tok_rows
+    visible = token <= limit
+    own_rows = group_rows // per_group
+
+    for g in range(KV):
+        heads = slice(g * HEAD, (g + 1) * HEAD)
+        query = jnp.concatenate(
+            [
+                q_all[g * per_group + j][:, h * HEAD : (h + 1) * HEAD]
+                for j in range(per_group)
+                for h in range(share // HEAD)
+            ],
+            axis=0,
+        )
+        scores = lax.dot_general(
+            query,
+            key_rows[:, heads],
+            (((1,), (1,)), ((), ())),
+            preferred_element_type=jnp.float32,
+        ) * HEAD ** (-0.5)
+        scores = jnp.where(visible, scores, -1e30)
+        peak = jnp.max(scores, axis=1, keepdims=True)
+        weights = jnp.where(visible, jnp.exp(scores - peak), 0.0)
+        total = jnp.sum(weights, axis=1, keepdims=True)
+        summed = jnp.dot(
+            weights.astype(jnp.bfloat16), value_rows[:, heads], preferred_element_type=jnp.float32
+        )
+        some = total > 0.0
+        total = jnp.where(some, total, 1.0)
+        level = jnp.where(some, peak + jnp.log(total), -1e30)
+        l_send[g] = jnp.transpose(jnp.broadcast_to(level, (group_rows, HEAD)))[0:8, :]
+        part = (summed / total).astype(jnp.bfloat16)
+        for j in range(per_group):
+            dest = g * per_group + j
+            o_send[dest] = part[j * own_rows : (j + 1) * own_rows, :]
+
+            @pl.when(me != dest)
+            def _():
+                peer_copy(3, dest, me, o_send.at[dest], o_recv).start()
+                peer_copy(4, dest, me, l_send.at[g], l_recv).start()
+
+    o_of = lambda peer: o_send.at[peer]
+    l_of = lambda peer: l_send.at[peer // per_group]
+    o_recv[me] = o_send[me]
+    l_recv[me] = l_send[me // per_group]
+    arrive(4, l_of, l_recv)
+    lmat[...] = jnp.zeros_like(lmat)
+    for j in range(n):
+        lmat[j : j + 1, :] = l_recv[j][0:1, :]
+    levels = lmat[0:n, :]
+    mass = jnp.exp(levels - jnp.max(levels, axis=0, keepdims=True))
+    lmat[0:n, :] = mass / jnp.sum(mass, axis=0, keepdims=True)
+    tmat[...] = jnp.transpose(lmat[...])
+    factor = tmat[pl.ds(pl.multiple_of((me % per_group) * own_rows, own_rows), own_rows), :]
+    arrive(3, o_of, o_recv)
+    attended = jnp.zeros((own_rows, HEAD), jnp.float32)
+    for j in range(n):
+        attended = attended + factor[:, j : j + 1] * o_recv[j].astype(jnp.float32)
+    mixed = jnp.concatenate(
+        [attended[0:scored_count], attended[scored_count:own_rows]], axis=1
+    ).astype(jnp.bfloat16)
+
+    chunk_lanes = wo.shape[1] // n
+    for c in range(n):
+        chunk = jnp.dot(
+            mixed, wo[:, pl.ds(c * chunk_lanes, chunk_lanes)], preferred_element_type=jnp.float32
+        )
+        for j in range(n):
+            f_rows[j, c : c + 1, :] = chunk[j : j + 1, :]
+    f_of = lambda peer: f_send.at[peer]
+
+    @pl.loop(0, n)
+    def _(j):
+        f_send[j] = f_rows[j].astype(jnp.bfloat16)
+
+    exchange(5, f_of, f_recv)
+    f_recv[me] = f_send[me]
+    sent(0, row_of, row_recv)
+    sent(1, pq_of, pq_recv)
+    sent(2, q_of, q_all)
+    sent(3, o_of, o_recv)
+    sent(4, l_of, l_recv)
+    for d in range(2):
+        ring_copy(d, 0, w_hbm[d]).wait_send()
+        core_copy(d, 0, core, w_hbm[d]).wait_send()
+
+        @pl.loop(1, RING)
+        def _(k):
+            @pl.when(k < RING - 1)
+            def _():
+                ring_copy(d, k).wait_send()
+
+            y_copy(d, k, y_rows).wait_send()
+            core_copy(d, k, core).wait_send()
+
+    arrive(5, f_of, f_recv)
+    result = f_recv[0].astype(jnp.float32)
+    for j in range(1, n):
+        result = result + f_recv[j].astype(jnp.float32)
+    out_ref[...] = result.astype(jnp.bfloat16)
+    sent(5, f_of, f_recv)
+
+
+def fused(hidden, norm_gain, w_query, b_query, w_key, w_value, b_value, w_out, step_ends):
+    n = lax.axis_size("tp")
+    me = lax.axis_index("tp")
+    tok_rows, width = hidden.shape
+    offset = lax.dynamic_slice_in_dim(step_ends, me, 1, 0)[0] - me * tok_rows
+    own_row = lax.dynamic_slice_in_dim(hidden, offset, 1, 0).astype(jnp.float32)
+    block, kv_cols = w_key.shape
+    share = w_query.shape[1] // n
+    chunk = w_out.shape[1] // n
+    bf16, f32 = jnp.bfloat16, jnp.float32
+    vmem = pl.BlockSpec(memory_space=pltpu.VMEM)
+    far = pl.BlockSpec(memory_space=pl.ANY)
+    dma = pltpu.SemaphoreType.DMA
+    own_rows = n * (share // HEAD)
+    out = pl.pallas_call(
+        kernel,
+        out_shape=jax.ShapeDtypeStruct((n, chunk), bf16),
+        in_specs=[vmem, pl.BlockSpec(memory_space=pltpu.SMEM), vmem, vmem, vmem] + [far] * 5,
+        out_specs=vmem,
+        scratch_shapes=[
+            pltpu.VMEM((tok_rows, width), bf16),
+            pltpu.VMEM((2, n, block, kv_cols), bf16),
+            pltpu.VMEM((2, tok_rows, kv_cols), f32),
+            pltpu.VMEM(w_query.shape, bf16),
+            pltpu.VMEM(w_out.shape, bf16),
+            pltpu.VMEM((n, 1, block), f32),
+            pltpu.VMEM((n, 1, block), f32),
+            pltpu.VMEM((n, block), f32),
+            pltpu.VMEM((n, n, share), f32),
+            pltpu.VMEM((n, n, share), f32),
+            pltpu.VMEM((n, n, share), bf16),
+            pltpu.VMEM((n, own_rows, HEAD), bf16),
+            pltpu.VMEM((n, own_rows, HEAD), bf16),
+            pltpu.VMEM((KV, 8, HEAD), f32),
+            pltpu.VMEM((n, 8, HEAD), f32),
+            pltpu.VMEM((HEAD, HEAD), f32),
+            pltpu.VMEM((HEAD, HEAD), f32),
+            pltpu.VMEM((n, n, chunk), f32),
+            pltpu.VMEM((n, n, chunk), bf16),
+            pltpu.VMEM((n, n, chunk), bf16),
+            dma((5,)),
+            dma((2, RING)),
+            dma((2, RING)),
+            dma((2, RING)),
+            dma((2, RING)),
+            dma((2, RING)),
+            dma((2, RING)),
+            dma((6, n)),
+            dma((6, n)),
+        ],
+        compiler_params=pltpu.CompilerParams(
+            collective_id=0, has_side_effects=True, vmem_limit_bytes=54 * 2**20
+        ),
+    )(
+        own_row,
+        step_ends,
+        norm_gain.reshape(1, -1),
+        b_query.reshape(1, -1),
+        b_value.reshape(1, -1),
+        hidden,
+        w_query,
+        w_key,
+        w_value,
+        w_out,
+    )
+    return out.reshape(1, n * chunk)
+
+
 def solution(mesh):
     in_specs = (
         P(("groups", "tp"), None),
@@ -91,4 +514,11 @@
         P("groups"),
     )
     out_specs = P(("groups", "tp"), None)
-    return jax.shard_map(shards, mesh=mesh, in_specs=in_specs, out_specs=out_specs, check_vma=False)
+    small = (mesh.shape["groups"], mesh.shape["tp"]) == (2, 16)
+    return jax.shard_map(
+        fused if small else shards,
+        mesh=mesh,
+        in_specs=in_specs,
+        out_specs=out_specs,
+        check_vma=False,
+    )

time: 470 us -> 104 us (0.22)
  blocking collectives: 208 us -> 0 us
  waiting for transfers between devices: 194 us -> 0 us
  Pallas kernels: 0 us -> 99.1 us
  matrix products: 27.7 us -> 0 us
  other arithmetic: 20.3 us -> 1.55 us
  between operations: 13.9 us -> 0.67 us
    unnamed x2 -> x0, blocking collectives: 122 us -> none
    pallas_call x0 -> x1, Pallas kernels: none -> 99.1 us  [fused(): pl.pallas_call(kernel, out_shape=jax.ShapeDtypeStruct((n, chunk), bf16),...]
    psum x1 -> x0, waiting for transfers between devices: 84 us -> none  [shards(): queries = (lax.psum(partial_query, 'tp') + b_query).astype(jnp.bfloat16)]
    all_gather x2 -> x0, waiting for transfers between devices: 81.4 us -> none  [the longest x1 76.6 us: shards(): lax.all_gather(w_key, 'tp', axis=0, tiled=True)]
    pmax x1 -> x0, blocking collectives: 60.7 us -> none  [shards(): global_peak = lax.pmax(local_peak, 'tp')]
    unnamed x5 -> x0, waiting for transfers between devices: 28.4 us -> none
    dot_general x6 -> x0, matrix products: 27.7 us -> none  [the longest x1 10.3 us: shards(): jnp.dot(normal_rows, lax.all_gather(w_value, 'tp', axis=0, tiled=True), p...]
    all_to_all x2 -> x0, blocking collectives: 25.1 us -> none  [the longest x1 13.7 us: shards(): lax.all_to_all(own_scored, 'tp', split_axis=1, concat_axis=0, tiled=True)]
  transfers between devices with their start and end apart: 4 -> 0, of which waited for: 4 -> 0; matrix products, arithmetic and copies ran while one was open for 3% -> 0% of each run, Pallas kernels for 0% -> 0%
where the time goes in v1:
time: 104 us
  Pallas kernels  99.1 us (95%)
  local copies, waits for them, and re-layouts  2.59 us (2%)
  other arithmetic  1.55 us (1%)
    pallas_call x1, Pallas kernels, fused(): pl.pallas_call(kernel, out_shape=jax.ShapeDtypeStruct((n, chunk), bf16),...  99.1 us

profile of v1, /device:TPU:0, one launch (start us, length us, event | category | flops | bytes accessed | tf_op | source)
XLA Modules:
  0.0 103.9 jit_solution(9066192720889517818)
XLA Ops:
  0.0 1.2 %dynamic_slice.6 = s32[1]{0:T(128)} dynamic-slice(s32[16]{0:T(128)} %ends_ref.1, s32[]{:T(128)S(6)} %select_n.6), dynamic_slice_sizes={1} | dynamic-slice | bytes 12 | tf_op jit(solution)/shard_map/dynamic_slice | solution.py:440
  1.9 1.6 %dynamic-slice_convert_fusion.row_ref = f32[1,8192]{1,0:T(1,128)} fusion(bf16[512,8192]{1,0:T(8,128)(2,1)} %hidden_ref.1, s32[]{:T(128)S(6)} %select_n.7), kind=kLoop, calls=%fused_computation | loop fusion | flops 8192 | bytes 49156 | tf_op jit(solution)/shard_map/convert_element_type | solution.py:441
  3.4 99.1 %shard_map.91 = bf16[16,512]{1,0:T(8,128)(2,1)} custom-call(f32[1,8192]{1,0:T(1,128)} %dynamic-slice_convert_fusion.row_ref, s32[16]{0:T(128)} %ends_ref.1, f32[1,8192]{1,0:T(1,128)} %bitcast.8, f32[1,4096]{1,0:T(1,128)} %bitcast.9, f32[1,512]{1,0:T(1,128)} %bitcast.10, bf16[512,8192]{1,0:T(8,128)(2,1)} %hidden_ref.1, bf16[512,4096]{1,0:T(8,128)(2,1)} %wq_hbm.1, ...), custom_call_target="tpu_custom_call" | custom-call | tf_op jit(solution)/shard_map/pallas_call | solution.py:450
  102.5 1.4 %copy.10 = bf16[1,1,16,512]{3,1,2,0:T(2,128)(2,1)} copy(bf16[1,1,16,512]{3,2,1,0:T(8,128)(2,1)} %bitcast.7) | data formatting | bytes 32768

commit v2 on v1

--- a/solution.py
+++ b/solution.py
@@ -83,16 +83,17 @@
 
 RING = 8
 SPLIT = 176
+LAST = 64
 NORM_ROWS = 32
 
 
 def kernel(
-    row_ref, ends_ref, gain_ref, bq_ref, bv_ref, hidden_ref, wq_hbm, wk_hbm, wv_hbm, wo_hbm,
+    ends_ref, gain_ref, bq_ref, bv_ref, hidden_ref, wq_hbm, wk_hbm, wv_hbm, wo_hbm,
     out_ref,
-    normal, held, acc, wq, wo, row_send, row_recv, cols, pq_send, pq_recv, q_all,
+    normal, own_row, held, acc, wq, wo, row_send, row_recv, cols, pq_send, pq_pair, pq_recv, q_all,
     o_send, o_recv, l_send, l_recv, lmat, tmat, f_rows, f_send, f_recv,
     load_sem, ring_send, ring_recv, y_send, y_recv, core_send, core_recv,
-    a2a_send, a2a_recv,
+    a2a_send, a2a_recv, pair_send, pair_recv,
 ):
     n = 16
     me = lax.axis_index("tp")
@@ -104,8 +105,6 @@
     pos = z * (1 - x) + (RING - 1 - z) * x
     partner = chip * 2 + 1 - core
     block = wk_hbm.shape[0]
-    ring_rows = pl.ds(pl.multiple_of(y * SPLIT, 16), block - SPLIT)
-    y_rows = pl.ds(pl.multiple_of(y * (block - SPLIT), 16), SPLIT)
     w_hbm = (wk_hbm, wv_hbm)
 
     def chip_at(p):
@@ -116,30 +115,32 @@
     def origin(d, k, c):
         return chip_at(pos + (2 * d - 1) * k) * 2 + c
 
-    def ring_copy(d, k, src=None):
-        slot = origin(d, k, core)
+    def rows_of(part):
+        if part == 0:
+            return pl.ds(pl.multiple_of(y * (block - SPLIT), 16), SPLIT)
+        if part == 1:
+            return pl.ds(SPLIT, block - 2 * SPLIT)
+        return pl.ds(pl.multiple_of((1 - y) * (block - SPLIT) + LAST, 16), SPLIT - LAST)
+
+    def ring_part(d, k, part, slot, src):
         return pltpu.make_async_remote_copy(
-            src_ref=held.at[d, slot, ring_rows] if src is None else src.at[ring_rows],
-            dst_ref=held.at[d, slot, ring_rows],
-            send_sem=ring_send.at[d, k],
-            recv_sem=ring_recv.at[d, k],
+            src_ref=(held.at[d, slot] if src is None else src).at[rows_of(part)],
+            dst_ref=held.at[d, slot, rows_of(part)],
+            send_sem=ring_send.at[part, d, k],
+            recv_sem=ring_recv.at[part, d, k],
             device_id={"tp": chip_at(pos + (1 - 2 * d)) * 2 + core},
             device_id_type=MESH,
         )
 
-    def ring_arrival(d, k):
-        slot = origin(d, k + 1, core)
-        return pltpu.make_async_remote_copy(
-            src_ref=held.at[d, slot, ring_rows],
-            dst_ref=held.at[d, slot, ring_rows],
-            send_sem=ring_send.at[d, k],
-            recv_sem=ring_recv.at[d, k],
-            device_id={"tp": chip_at(pos + (1 - 2 * d)) * 2 + core},
-            device_id_type=MESH,
-        )
-
-    def y_copy(d, k, rows):
+    def ring_copy(d, k, part, src=None):
+        return ring_part(d, k, part, origin(d, k, core), src)
+
+    def ring_arrival(d, k, part):
+        return ring_part(d, k, part, origin(d, k + 1, core), None)
+
+    def y_copy(d, k, owner, count=SPLIT):
         slot = origin(d, k, core)
+        rows = pl.ds(pl.multiple_of(owner * (block - SPLIT), 16), count)
         return pltpu.make_async_remote_copy(
             src_ref=held.at[d, slot, rows],
             dst_ref=held.at[d, slot, rows],
@@ -148,8 +149,6 @@
             device_id={"groups": 1 - y},
             device_id_type=MESH,
         )
-
-    peer_rows = pl.ds(pl.multiple_of((1 - y) * (block - SPLIT), 16), SPLIT)
 
     def core_copy(d, k, c, src=None):
         slot = origin(d, k, c)
@@ -205,23 +204,15 @@
     pl.semaphore_signal(barrier, inc=1, device_id={"groups": 1 - y}, device_id_type=MESH)
     pl.semaphore_wait(barrier, n)
 
-    for d in range(2):
-        ring_copy(d, 0, w_hbm[d]).start()
+    for part in range(2):
+        for d in range(2):
+            ring_copy(d, 0, part, w_hbm[d]).start()
     for d in range(2):
         core_copy(d, 0, core, w_hbm[d]).start()
 
-    row = row_ref[...]
-    row_scale = lax.rsqrt(jnp.sum(row * row, axis=-1, keepdims=True) / row.shape[1] + 1e-06)
-    for j in range(n):
-        part = pl.ds(j * block, block)
-        piece = row_ref[:, part] * row_scale * gain_ref[:, part]
-        row_send[j] = piece.astype(jnp.bfloat16).astype(jnp.float32)
-    row_recv[pl.ds(me, 1)] = row_send[pl.ds(me, 1)]
     row_of = lambda peer: row_send.at[peer]
-    exchange(0, row_of, row_recv)
-    for load in loads:
-        load.wait()
-
+    tok_rows = normal.shape[0]
+    offset = ends_ref[me] % tok_rows
     width = normal.shape[1]
     piece_lanes = 256
 
@@ -229,6 +220,7 @@
         @pl.loop(first, last)
         def _(i):
             rows = pl.ds(pl.multiple_of(i * NORM_ROWS, NORM_ROWS), NORM_ROWS)
+            picked = i * NORM_ROWS + lax.broadcasted_iota(jnp.int32, (NORM_ROWS, 1), 0) == offset
             squares = jnp.zeros((NORM_ROWS, piece_lanes), jnp.float32)
             for c in range(0, width, piece_lanes):
                 v = normal[rows, pl.ds(c, piece_lanes)].astype(jnp.float32)
@@ -237,12 +229,12 @@
             for c in range(0, width, piece_lanes):
                 lanes = pl.ds(c, piece_lanes)
                 v = normal[rows, lanes].astype(jnp.float32)
-                normal[rows, lanes] = (v * scale * gain_ref[:, lanes]).astype(jnp.bfloat16)
-
-    tok_rows = normal.shape[0]
+                rounded = (v * scale * gain_ref[:, lanes]).astype(jnp.bfloat16)
+                normal[rows, lanes] = rounded
+                own = jnp.where(picked, rounded.astype(jnp.float32), 0.0)
+                own_row[:, lanes] += own[0:8] + own[8:16] + own[16:24] + own[24:32]
+
     steps = tok_rows // NORM_ROWS
-    norm_rows(0, steps // 2)
-    acc[...] = jnp.zeros_like(acc)
 
     def project(k, c):
         @pl.loop(0, 2)
@@ -254,27 +246,66 @@
             )
 
     share = wq.shape[1] // n
-    pq_of = lambda peer: pq_send.at[peer]
-    q_of = lambda peer: q_all.at[me]
-
-    @pl.loop(0, RING - 1)
+
+    def chip_copy(phase, other, slot, send, recv):
+        return pltpu.make_async_remote_copy(
+            src_ref=send,
+            dst_ref=recv.at[slot],
+            send_sem=a2a_send.at[phase, other],
+            recv_sem=a2a_recv.at[phase, slot],
+            device_id={"tp": other * 2 + core},
+            device_id_type=MESH,
+        )
+
+    def for_chips(body):
+        @pl.loop(1, RING)
+        def _(k):
+            body((chip + k) % RING)
+
+    def pair_copy(phase, send, recv):
+        return pltpu.make_async_remote_copy(
+            src_ref=send,
+            dst_ref=recv,
+            send_sem=pair_send.at[phase],
+            recv_sem=pair_recv.at[phase],
+            device_id={"tp": partner},
+            device_id_type=MESH,
+        )
+
+    pq_of = lambda other: pq_send.at[core, other]
+    q_of = lambda other: q_all.at[core, chip]
+    pq_swap = lambda: pair_copy(0, pq_send.at[1 - core], pq_pair)
+    q_swap = lambda c: pair_copy(1, q_all.at[c], q_all.at[c])
+
+    @pl.loop(0, RING - 2)
     def _(s):
-        for d in range(2):
-            ring_arrival(d, s).wait_recv()
-
-            @pl.when(s < RING - 2)
-            def _():
-                ring_copy(d, s + 1).start()
-
-            y_copy(d, s + 1, y_rows).start()
+        for part in range(2):
+            for d in range(2):
+                ring_arrival(d, s, part).wait_recv()
+                ring_copy(d, s + 1, part).start()
+                if part == 0:
+                    y_copy(d, s + 1, y).start()
 
         @pl.when(s >= 1)
         def _():
             for d in range(2):
-                y_copy(d, s, peer_rows).wait_recv()
+                y_copy(d, s, 1 - y).wait_recv()
                 core_copy(d, s, core).start()
 
         @pl.when(s == 0)
+        def _():
+            acc[...] = jnp.zeros_like(acc)
+            own_row[...] = jnp.zeros_like(own_row)
+            for load in loads:
+                load.wait()
+            norm_rows(0, steps)
+            for j in range(n):
+                row_send[j] = jnp.sum(own_row[:, pl.ds(j * block, block)], axis=0, keepdims=True)
+            row_recv[pl.ds(me, 1)] = row_send[pl.ds(me, 1)]
+            exchange(0, row_of, row_recv)
+            project(0, core)
+
+        @pl.when(s == 1)
         def _():
             arrive(0, row_of, row_recv)
             for j in range(n):
@@ -283,26 +314,37 @@
 
             @pl.loop(0, n)
             def _(j):
-                pq_send[j] = jnp.dot(
+                pq_send[j % 2, j // 2] = jnp.dot(
                     scored,
                     wq[:, pl.ds(pl.multiple_of(j * share, share), share)],
                     preferred_element_type=jnp.float32,
                 )
 
-            pq_recv[pl.ds(me, 1)] = pq_send[pl.ds(me, 1)]
-            exchange(1, pq_of, pq_recv)
-            norm_rows(steps // 2, steps)
-            project(0, core)
-
-        @pl.when(s == 1)
-        def _():
-            arrive(1, pq_of, pq_recv)
+            pq_swap().start()
+
+        @pl.when(s == 2)
+        def _():
+            pq_swap().wait_recv()
+            pq_send[core] = pq_send[core] + pq_pair[...]
+            for_chips(lambda other: chip_copy(1, other, chip, pq_of(other), pq_recv).start())
+            pq_recv[chip] = pq_send[core, chip]
+
+        @pl.when(s == 3)
+        def _():
+            for_chips(lambda other: chip_copy(1, other, other, pq_of(other), pq_recv).wait_recv())
             total = pq_recv[0]
-            for j in range(1, n):
+            for j in range(1, RING):
                 total = total + pq_recv[j]
             bias = bq_ref[:, pl.ds(pl.multiple_of(me * share, share), share)]
-            q_all[me] = (total + bias).astype(jnp.bfloat16)
-            exchange(2, q_of, q_all)
+            q_all[core, chip] = (total + bias).astype(jnp.bfloat16)
+            for_chips(lambda other: chip_copy(2, other, chip, q_of(other), q_all.at[core]).start())
+
+        @pl.when(s == 4)
+        def _():
+            for_chips(
+                lambda other: chip_copy(2, other, other, q_of(other), q_all.at[core]).wait_recv()
+            )
+            q_swap(core).start()
 
         @pl.when(s >= 1)
         def _():
@@ -311,16 +353,32 @@
                 core_copy(d, s - 1, 1 - core).wait_recv()
             project(s - 1, 1 - core)
 
-    for d in range(2):
-        y_copy(d, RING - 1, peer_rows).wait_recv()
-        core_copy(d, RING - 1, core).start()
-    project(RING - 1, core)
-    for k in (RING - 2, RING - 1):
-        for d in range(2):
-            core_copy(d, k, 1 - core).wait_recv()
-        project(k, 1 - core)
-
-    arrive(2, q_of, q_all)
+    last = RING - 1
+    for d in range(2):
+        ring_arrival(d, last - 1, 0).wait_recv()
+        y_copy(d, last, y, LAST).start()
+    for d in range(2):
+        y_copy(d, last - 1, 1 - y).wait_recv()
+        ring_copy(d, last - 1, 2).start()
+        core_copy(d, last - 1, core).start()
+    project(last - 1, core)
+    for d in range(2):
+        core_copy(d, last - 2, 1 - core).wait_recv()
+    project(last - 2, 1 - core)
+    for d in range(2):
+        ring_arrival(d, last - 1, 1).wait_recv()
+        y_copy(d, last, 1 - y, LAST).wait_recv()
+        ring_arrival(d, last - 1, 2).wait_recv()
+        core_copy(d, last, core).start()
+    for d in range(2):
+        core_copy(d, last - 1, 1 - core).wait_recv()
+    project(last - 1, 1 - core)
+    project(last, core)
+    for d in range(2):
+        core_copy(d, last, 1 - core).wait_recv()
+    project(last, 1 - core)
+    q_swap(1 - core).wait_recv()
+
     key_rows = acc[0].astype(jnp.bfloat16)
     value_rows = (acc[1] + bv_ref[...]).astype(jnp.bfloat16)
     scored_count = n
@@ -338,7 +396,7 @@
         heads = slice(g * HEAD, (g + 1) * HEAD)
         query = jnp.concatenate(
             [
-                q_all[g * per_group + j][:, h * HEAD : (h + 1) * HEAD]
+                q_all[(g * per_group + j) % 2, (g * per_group + j) // 2][:, h * HEAD : (h + 1) * HEAD]
                 for j in range(per_group)
                 for h in range(share // HEAD)
             ],
@@ -408,22 +466,29 @@
     exchange(5, f_of, f_recv)
     f_recv[me] = f_send[me]
     sent(0, row_of, row_recv)
-    sent(1, pq_of, pq_recv)
-    sent(2, q_of, q_all)
+    for_chips(lambda other: chip_copy(1, other, chip, pq_of(other), pq_recv).wait_send())
+    for_chips(lambda other: chip_copy(2, other, chip, q_of(other), q_all.at[core]).wait_send())
+    pq_swap().wait_send()
+    q_swap(core).wait_send()
     sent(3, o_of, o_recv)
     sent(4, l_of, l_recv)
     for d in range(2):
-        ring_copy(d, 0, w_hbm[d]).wait_send()
+        for part in range(2):
+            ring_copy(d, 0, part, w_hbm[d]).wait_send()
         core_copy(d, 0, core, w_hbm[d]).wait_send()
 
         @pl.loop(1, RING)
         def _(k):
             @pl.when(k < RING - 1)
             def _():
-                ring_copy(d, k).wait_send()
-
-            y_copy(d, k, y_rows).wait_send()
+                for part in range(2):
+                    ring_copy(d, k, part).wait_send()
+                y_copy(d, k, y).wait_send()
+
             core_copy(d, k, core).wait_send()
+
+        ring_copy(d, last - 1, 2).wait_send()
+        y_copy(d, last, y, LAST).wait_send()
 
     arrive(5, f_of, f_recv)
     result = f_recv[0].astype(jnp.float32)
@@ -435,10 +500,7 @@
 
 def fused(hidden, norm_gain, w_query, b_query, w_key, w_value, b_value, w_out, step_ends):
     n = lax.axis_size("tp")
-    me = lax.axis_index("tp")
     tok_rows, width = hidden.shape
-    offset = lax.dynamic_slice_in_dim(step_ends, me, 1, 0)[0] - me * tok_rows
-    own_row = lax.dynamic_slice_in_dim(hidden, offset, 1, 0).astype(jnp.float32)
     block, kv_cols = w_key.shape
     share = w_query.shape[1] // n
     chunk = w_out.shape[1] // n
@@ -450,10 +512,11 @@
     out = pl.pallas_call(
         kernel,
         out_shape=jax.ShapeDtypeStruct((n, chunk), bf16),
-        in_specs=[vmem, pl.BlockSpec(memory_space=pltpu.SMEM), vmem, vmem, vmem] + [far] * 5,
+        in_specs=[pl.BlockSpec(memory_space=pltpu.SMEM), vmem, vmem, vmem] + [far] * 5,
         out_specs=vmem,
         scratch_shapes=[
             pltpu.VMEM((tok_rows, width), bf16),
+            pltpu.VMEM((8, width), f32),
             pltpu.VMEM((2, n, block, kv_cols), bf16),
             pltpu.VMEM((2, tok_rows, kv_cols), f32),
             pltpu.VMEM(w_query.shape, bf16),
@@ -461,9 +524,10 @@
             pltpu.VMEM((n, 1, block), f32),
             pltpu.VMEM((n, 1, block), f32),
             pltpu.VMEM((n, block), f32),
-            pltpu.VMEM((n, n, share), f32),
-            pltpu.VMEM((n, n, share), f32),
-            pltpu.VMEM((n, n, share), bf16),
+            pltpu.VMEM((2, n // 2, n, share), f32),
+            pltpu.VMEM((n // 2, n, share), f32),
+            pltpu.VMEM((n // 2, n, share), f32),
+            pltpu.VMEM((2, n // 2, n, share), bf16),
             pltpu.VMEM((n, own_rows, HEAD), bf16),
             pltpu.VMEM((n, own_rows, HEAD), bf16),
             pltpu.VMEM((KV, 8, HEAD), f32),
@@ -474,20 +538,21 @@
             pltpu.VMEM((n, n, chunk), bf16),
             pltpu.VMEM((n, n, chunk), bf16),
             dma((5,)),
-            dma((2, RING)),
-            dma((2, RING)),
+            dma((3, 2, RING)),
+            dma((3, 2, RING)),
             dma((2, RING)),
             dma((2, RING)),
             dma((2, RING)),
             dma((2, RING)),
             dma((6, n)),
             dma((6, n)),
+            dma((2,)),
+            dma((2,)),
         ],
         compiler_params=pltpu.CompilerParams(
             collective_id=0, has_side_effects=True, vmem_limit_bytes=54 * 2**20
         ),
     )(
-        own_row,
         step_ends,
         norm_gain.reshape(1, -1),
         b_query.reshape(1, -1),

time: 104 us -> 91.9 us (0.88)
  Pallas kernels: 99.1 us -> 90 us
  other arithmetic: 1.55 us -> 0 us
  local copies, waits for them, and re-layouts: 2.59 us -> 1.36 us
    pallas_call x1, Pallas kernels: 99.1 us -> 90 us  [fused(): pl.pallas_call(kernel, out_shape=jax.ShapeDtypeStruct((n, chunk), bf16),...]
    convert_element_type x1 -> x0, other arithmetic: 1.55 us -> none  [fused(): own_row = lax.dynamic_slice_in_dim(hidden, offset, 1, 0).astype(jnp.float32)]
    dynamic_slice x1 -> x0, local copies, waits for them, and re-layouts: 1.24 us -> none  [fused(): offset = lax.dynamic_slice_in_dim(step_ends, me, 1, 0)[0] - me * tok_rows]
where the time goes in v2:
time: 91.9 us; the launch traced here: 91.4 us
  Pallas kernels  90 us (98%)
  local copies, waits for them, and re-layouts  1.36 us (1%)
    pallas_call x1, Pallas kernels, fused(): pl.pallas_call(kernel, out_shape=jax.ShapeDtypeStruct((n, chunk), bf16),...  90 us

profile of v2, /device:TPU:0, one launch (start us, length us, event | category | flops | bytes accessed | tf_op | source)
XLA Modules:
  0.0 91.4 jit_solution(14079806594062279924)
XLA Ops:
  0.0 90.0 %shard_map.91 = bf16[16,512]{1,0:T(8,128)(2,1)} custom-call(s32[16]{0:T(128)} %ends_ref.1, f32[1,8192]{1,0:T(1,128)} %bitcast.7, f32[1,4096]{1,0:T(1,128)} %bitcast.8, f32[1,512]{1,0:T(1,128)} %bitcast.9, bf16[512,8192]{1,0:T(8,128)(2,1)} %hidden_ref.1, bf16[512,4096]{1,0:T(8,128)(2,1)} %wq_hbm.1, bf16[512,512]{1,0:T(8,128)(2,1)} %wk_hbm.1, ...), custom_call_target="tpu_custom_call" | custom-call | tf_op jit(solution)/shard_map/pallas_call | solution.py:512
  90.0 1.4 %copy.10 = bf16[1,1,16,512]{3,1,2,0:T(2,128)(2,1)} copy(bf16[1,1,16,512]{3,2,1,0:T(8,128)(2,1)} %bitcast.6) | data formatting | bytes 32768

commit v3 on v2

--- a/solution.py
+++ b/solution.py
@@ -115,12 +115,16 @@
     def origin(d, k, c):
         return chip_at(pos + (2 * d - 1) * k) * 2 + c
 
+    late = SPLIT - LAST
+    late_rows = pl.ds(pl.multiple_of((1 - y) * (block - late), 16), late)
+    early_rows = pl.ds(pl.multiple_of(y * late, 16), block - late)
+
     def rows_of(part):
         if part == 0:
             return pl.ds(pl.multiple_of(y * (block - SPLIT), 16), SPLIT)
         if part == 1:
             return pl.ds(SPLIT, block - 2 * SPLIT)
-        return pl.ds(pl.multiple_of((1 - y) * (block - SPLIT) + LAST, 16), SPLIT - LAST)
+        return late_rows
 
     def ring_part(d, k, part, slot, src):
         return pltpu.make_async_remote_copy(
@@ -140,13 +144,25 @@
 
     def y_copy(d, k, owner, count=SPLIT):
         slot = origin(d, k, core)
-        rows = pl.ds(pl.multiple_of(owner * (block - SPLIT), 16), count)
+        start = (1 - owner) * (SPLIT - count) + owner * (block - SPLIT)
+        rows = pl.ds(pl.multiple_of(start, 16), count)
         return pltpu.make_async_remote_copy(
             src_ref=held.at[d, slot, rows],
             dst_ref=held.at[d, slot, rows],
             send_sem=y_send.at[d, k],
             recv_sem=y_recv.at[d, k],
             device_id={"groups": 1 - y},
+            device_id_type=MESH,
+        )
+
+    def core_rows(d, c, rows, index):
+        slot = origin(d, RING - 1, c)
+        return pltpu.make_async_remote_copy(
+            src_ref=held.at[d, slot, rows],
+            dst_ref=held.at[d, slot, rows],
+            send_sem=core_send.at[d, index],
+            recv_sem=core_recv.at[d, index],
+            device_id={"tp": partner},
             device_id_type=MESH,
         )
 
@@ -368,14 +384,17 @@
     for d in range(2):
         ring_arrival(d, last - 1, 1).wait_recv()
         y_copy(d, last, 1 - y, LAST).wait_recv()
+        core_rows(d, core, early_rows, last).start()
+    for d in range(2):
         ring_arrival(d, last - 1, 2).wait_recv()
-        core_copy(d, last, core).start()
+        core_rows(d, core, late_rows, last + 1).start()
     for d in range(2):
         core_copy(d, last - 1, 1 - core).wait_recv()
     project(last - 1, 1 - core)
     project(last, core)
     for d in range(2):
-        core_copy(d, last, 1 - core).wait_recv()
+        core_rows(d, 1 - core, early_rows, last).wait_recv()
+        core_rows(d, 1 - core, late_rows, last + 1).wait_recv()
     project(last, 1 - core)
     q_swap(1 - core).wait_recv()
 
@@ -418,7 +437,7 @@
         some = total > 0.0
         total = jnp.where(some, total, 1.0)
         level = jnp.where(some, peak + jnp.log(total), -1e30)
-        l_send[g] = jnp.transpose(jnp.broadcast_to(level, (group_rows, HEAD)))[0:8, :]
+        l_send[g] = jnp.transpose(jnp.broadcast_to(level, (group_rows, HEAD)))[0:1, :]
         part = (summed / total).astype(jnp.bfloat16)
         for j in range(per_group):
             dest = g * per_group + j
@@ -436,7 +455,7 @@
     arrive(4, l_of, l_recv)
     lmat[...] = jnp.zeros_like(lmat)
     for j in range(n):
-        lmat[j : j + 1, :] = l_recv[j][0:1, :]
+        lmat[j : j + 1, :] = l_recv[j]
     levels = lmat[0:n, :]
     mass = jnp.exp(levels - jnp.max(levels, axis=0, keepdims=True))
     lmat[0:n, :] = mass / jnp.sum(mass, axis=0, keepdims=True)
@@ -484,9 +503,10 @@
                 for part in range(2):
                     ring_copy(d, k, part).wait_send()
                 y_copy(d, k, y).wait_send()
-
-            core_copy(d, k, core).wait_send()
-
+                core_copy(d, k, core).wait_send()
+
+        core_rows(d, core, early_rows, last).wait_send()
+        core_rows(d, core, late_rows, last + 1).wait_send()
         ring_copy(d, last - 1, 2).wait_send()
         y_copy(d, last, y, LAST).wait_send()
 
@@ -530,8 +550,8 @@
             pltpu.VMEM((2, n // 2, n, share), bf16),
             pltpu.VMEM((n, own_rows, HEAD), bf16),
             pltpu.VMEM((n, own_rows, HEAD), bf16),
-            pltpu.VMEM((KV, 8, HEAD), f32),
-            pltpu.VMEM((n, 8, HEAD), f32),
+            pltpu.VMEM((KV, 1, HEAD), f32),
+            pltpu.VMEM((n, 1, HEAD), f32),
             pltpu.VMEM((HEAD, HEAD), f32),
             pltpu.VMEM((HEAD, HEAD), f32),
             pltpu.VMEM((n, n, chunk), f32),
@@ -542,8 +562,8 @@
             dma((3, 2, RING)),
             dma((2, RING)),
             dma((2, RING)),
-            dma((2, RING)),
-            dma((2, RING)),
+            dma((2, RING + 1)),
+            dma((2, RING + 1)),
             dma((6, n)),
             dma((6, n)),
             dma((2,)),

time: 91.9 us -> 90.5 us (0.985)
  Pallas kernels: 90 us -> 88.3 us
    pallas_call x1, Pallas kernels: 90 us -> 88.3 us  [fused(): pl.pallas_call(kernel, out_shape=jax.ShapeDtypeStruct((n, chunk), bf16),...]
where the time goes in v3:
time: 90.5 us; the launch traced here: 89.7 us
  Pallas kernels  88.3 us (98%)
  local copies, waits for them, and re-layouts  1.36 us (2%)
    pallas_call x1, Pallas kernels, fused(): pl.pallas_call(kernel, out_shape=jax.ShapeDtypeStruct((n, chunk), bf16),...  88.3 us

profile of v3, /device:TPU:0, one launch (start us, length us, event | category | flops | bytes accessed | tf_op | source)
XLA Modules:
  0.0 89.7 jit_solution(13264600072558953102)
XLA Ops:
  0.0 88.3 %shard_map.91 = bf16[16,512]{1,0:T(8,128)(2,1)} custom-call(s32[16]{0:T(128)} %ends_ref.1, f32[1,8192]{1,0:T(1,128)} %bitcast.7, f32[1,4096]{1,0:T(1,128)} %bitcast.8, f32[1,512]{1,0:T(1,128)} %bitcast.9, bf16[512,8192]{1,0:T(8,128)(2,1)} %hidden_ref.1, bf16[512,4096]{1,0:T(8,128)(2,1)} %wq_hbm.1, bf16[512,512]{1,0:T(8,128)(2,1)} %wk_hbm.1, ...), custom_call_target="tpu_custom_call" | custom-call | tf_op jit(solution)/shard_map/pallas_call | solution.py:532
  88.3 1.4 %copy.10 = bf16[1,1,16,512]{3,1,2,0:T(2,128)(2,1)} copy(bf16[1,1,16,512]{3,2,1,0:T(8,128)(2,1)} %bitcast.6) | data formatting | bytes 32768
